TPU v7x, 32 devices: a whole 2x2x4 slice. The times are simulated.
32 devices in a mesh: dp: 4 (over y, core), space: 8 (over z, x).
Axes of the slice: x: 2, y: 2, z: 4, core: 2. Of those that a mesh axis runs over, the one named last changes fastest.
Arguments:
- snapshot: bfloat16 [4, 32, 64, 1024], P('dp', 'space'), may hold values from -6 to 6
- conv_one: bfloat16 [864, 128], replicated, may hold values from -0.21875 to 0.21875
- conv_two: bfloat16 [3456, 256], replicated, may hold values from -0.0546875 to 0.0546875
- cotangent: bfloat16 [4, 256, 8, 128], P('dp', 'space'), may hold values from -0.046875 to 0.046875
Outputs:
- latent: bfloat16 [4, 256, 8, 128], P('dp', 'space')
- grad_one: float32 [128, 864], P('space')
- grad_two: float32 [256, 3456], P('space')
All inputs are finite; a program needn't handle non-finite values.
Results may differ from a plain program's by a relative error of at most 0.0049.
Values may be sent and summed in bfloat16 or wider, within the bound.
No kernel may reach another device: no remote copies, remote signals or barrier semaphores. Data moves between devices by JAX's collectives and lax.ppermute only.
A program may use at most 64 MiB of HBM per device.

v0:
```python
import jax
import jax.numpy as jnp
from jax import lax
from jax.sharding import PartitionSpec as P


def from_behind(block, axis, distance):
    devices = range(lax.axis_size(axis))
    route = [(i - distance, i) for i in devices if i - distance in devices]
    return lax.ppermute(block, axis, route)


def patches(padded, out_x, out_y, out_z):
    channels = padded.shape[3]
    grown = jnp.pad(padded, ((0, 1), (0, 1), (0, 1), (0, 0)))
    phased = grown.reshape(out_x + 1, 2, out_y + 1, 2, out_z + 1, 2, channels)
    pieces = []
    for tap_x in range(3):
        for tap_y in range(3):
            for tap_z in range(3):
                start = (tap_x // 2, tap_x % 2, tap_y // 2, tap_y % 2, tap_z // 2, tap_z % 2, 0)
                limit = (
                    tap_x // 2 + out_x,
                    tap_x % 2 + 1,
                    tap_y // 2 + out_y,
                    tap_y % 2 + 1,
                    tap_z // 2 + out_z,
                    tap_z % 2 + 1,
                    channels,
                )
                pieces.append(
                    lax.slice(phased, start, limit).reshape(out_x, out_y, out_z, channels)
                )
    stacked = jnp.concatenate(pieces, axis=3)
    return stacked.reshape(out_x * out_y * out_z, 27 * channels)


def fold_axis(blocks, space, tap):
    first_tap = lax.index_in_dim(blocks, 0, tap, keepdims=False)
    middle_tap = lax.index_in_dim(blocks, 1, tap, keepdims=False)
    last_tap = lax.index_in_dim(blocks, 2, tap, keepdims=False)
    after = [(0, 0)] * first_tap.ndim
    before = [(0, 0)] * first_tap.ndim
    after[space] = (0, 1)
    before[space] = (1, 0)
    even_cells = jnp.pad(first_tap, after) + jnp.pad(last_tap, before)
    odd_cells = jnp.pad(middle_tap, after)
    joined = jnp.stack([even_cells, odd_cells], axis=space + 1)
    shape = list(even_cells.shape)
    shape[space] = 2 * shape[space]
    return joined.reshape(shape)


def spread_taps(back_rows, out_x, out_y, out_z):
    channels = back_rows.shape[1] // 27
    blocks = back_rows.reshape(out_x, out_y, out_z, 3, 3, 3, channels)
    blocks = fold_axis(blocks, 2, 5)
    blocks = fold_axis(blocks, 1, 4)
    blocks = fold_axis(blocks, 0, 3)
    return blocks[: 2 * out_x + 1, : 2 * out_y + 1, : 2 * out_z + 1]


def silu_slope(values):
    logistic = jax.nn.sigmoid(values)
    return logistic * (1.0 + values * (1.0 - logistic))


def on_device(snapshot, conv_one, conv_two, cotangent):
    in_width = conv_one.shape[0] // 27
    mid_width = conv_one.shape[1]
    out_width = conv_two.shape[1]
    slab_cells = snapshot[0]
    extent_x, extent_y = (slab_cells.shape[0], slab_cells.shape[1])
    fine_grid = slab_cells.reshape(extent_x, extent_y, -1, in_width)
    extent_z = fine_grid.shape[2]
    half_x, half_y, half_z = (extent_x // 2, extent_y // 2, extent_z // 2)
    quarter_x, quarter_y, quarter_z = (extent_x // 4, extent_y // 4, extent_z // 4)
    lower_plane = from_behind(slab_cells[extent_x - 1 :], "space", 1)
    joined = jnp.concatenate(
        [lower_plane.reshape(1, extent_y, extent_z, in_width), fine_grid], axis=0
    )
    padded = jnp.pad(joined, ((0, 0), (1, 0), (1, 0), (0, 0)))
    patch_one = patches(padded, half_x, half_y, half_z)
    hidden_pre = jnp.dot(patch_one, conv_one, preferred_element_type=jnp.float32)
    hidden = jax.nn.silu(hidden_pre).astype(jnp.bfloat16)
    act_grid = hidden.reshape(half_x, half_y, half_z, mid_width)
    act_lower = from_behind(act_grid[half_x - 1 :], "space", 1)
    act_pad = jnp.pad(
        jnp.concatenate([act_lower, act_grid], axis=0), ((0, 0), (1, 0), (1, 0), (0, 0))
    )
    patch_two = patches(act_pad, quarter_x, quarter_y, quarter_z)
    latent_rows = jnp.dot(patch_two, conv_two, preferred_element_type=jnp.float32).astype(
        jnp.bfloat16
    )
    latent_slab = latent_rows.reshape(quarter_x, -1, out_width).transpose(2, 0, 1)
    latent = lax.all_to_all(latent_slab, "space", split_axis=0, concat_axis=1, tiled=True)[None]
    upstream = lax.all_to_all(cotangent[0], "space", split_axis=1, concat_axis=0, tiled=True)
    grad_grid = upstream.transpose(1, 2, 0)
    grad_rows = grad_grid.reshape(-1, out_width)
    term_two = lax.dot_general(
        patch_two, grad_rows, (((0,), (0,)), ((), ())), preferred_element_type=jnp.float32
    ).T
    back_rows = lax.dot_general(
        grad_rows, conv_two, (((1,), (1,)), ((), ())), preferred_element_type=jnp.float32
    )
    grad_pad = spread_taps(back_rows, quarter_x, quarter_y, quarter_z)
    upper_plane = from_behind(grad_pad[0:1, 1:, 1:], "space", -1)
    grad_act = jnp.concatenate(
        [grad_pad[1:half_x, 1:, 1:], grad_pad[half_x:, 1:, 1:] + upper_plane], axis=0
    )
    grad_pre = (grad_act.reshape(-1, mid_width) * silu_slope(hidden_pre)).astype(jnp.bfloat16)
    term_one = lax.dot_general(
        patch_one, grad_pre, (((0,), (0,)), ((), ())), preferred_element_type=jnp.float32
    ).T
    summed = lax.psum((term_one, term_two), "dp")
    shares = (
        lax.psum_scatter(summed[0], "space", scatter_dimension=0, tiled=True),
        lax.psum_scatter(summed[1], "space", scatter_dimension=0, tiled=True),
    )
    return (latent, shares[0], shares[1])


def solution(mesh):
    placed = (P("dp", "space", None, None), P(), P(), P("dp", "space", None, None))
    return jax.shard_map(
        on_device,
        mesh=mesh,
        in_specs=placed,
        out_specs=(P("dp", "space", None, None), P("space", None), P("space", None)),
        check_vma=False,
    )
```

profile of v0, /device:TPU:0, one launch (start us, length us, event | category | flops | bytes accessed | tf_op | source)
XLA Modules:
  0.0 328.7 jit_solution(645473647259848543)
XLA Ops:
  7.2 1.6 copy.254
  8.8 7.3 %all-to-all-start.1 = ((bf16[32,8,128]{2,0,1:T(8,128)(2,1)}), bf16[32,8,128]{2,0,1:T(8,128)(2,1)S(1)}, u32[]{:S(2)}, u32[]{:S(2)}) async-start(bf16[32,8,128]{2,0,1:T(8,128)(2,1)} %bitcast.179), calls=%async_computation.1 | async-start | bytes 131072 | tf_op jit(solution)/shard_map/all_to_all | solution.py:97
  16.1 1.5 copy.144
  17.6 0.7 slice_bitcast_fusion.9
  18.3 3.9 %collective-permute-start = (bf16[1,64,1024]{1,2,0:T(8,128)(2,1)}, bf16[1,64,1024]{1,2,0:T(8,128)(2,1)S(1)}, u32[]{:S(2)}, u32[]{:S(2)}) collective-permute-start(bf16[1,64,1024]{1,2,0:T(8,128)(2,1)} %slice_bitcast_fusion.9), channel_id=1, source_target_pairs={{0,1},{1,2},{2,3},{3,4},{4,5},{5,6},{6,7},{8,9},{9,10},{10,11},{11... | collective-permute-start | bytes 393224 | tf_op jit(solution)/shard_map/ppermute | solution.py:10
  22.2 0.7 all-to-all-done.1
  23.1 0.7 convolution_bitcast_fusion.1
  24.3 0.4 copy.181
  25.1 1.0 copy.184
  26.0 0.6 slice_bitcast_fusion.8
  26.9 0.5 add_bitcast_fusion.2
  27.4 0.5 pad_maximum_fusion.3
  27.9 0.6 copy.185
  28.6 1.0 copy-done.3
  29.6 1.2 fusion.11
  30.8 1.5 collective-permute-start.2
  32.3 1.3 pad_maximum_fusion.2
  33.6 3.9 %copy.225 = bf16[5,64,32,32]{3,1,2,0:T(8,128)(2,1)} copy(bf16[5,64,32,32]{1,3,2,0:T(8,128)(2,1)} %pad_maximum_fusion.2) | data formatting | bytes 1310720
  37.6 4.9 %pad.74 = bf16[6,66,34,32]{3,1,2,0:T(8,128)(2,1)} pad(bf16[5,64,32,32]{3,1,2,0:T(8,128)(2,1)} %copy.225, bf16[]{:T(256)} %constant.6.clone.1), padding=0_1x1_1x1_1x0_0 | pad | bytes 1517058 | tf_op jit(solution)/shard_map/jit(_pad)/pad | solution.py:15
  42.4 8.2 %reshape.213 = bf16[3,2,33,2,17,2,32]{6,3,2,5,4,1,0:T(2,128)(2,1)} reshape(bf16[6,66,34,32]{3,1,2,0:T(8,128)(2,1)} %pad.74) | data formatting | bytes 1723392 | tf_op jit(solution)/shard_map/reshape | solution.py:16
  50.6 15.0 %fusion.9 = (bf16[2,1,32,1,16,1,32]{6,3,2,5,4,1,0:T(2,128)(2,1)S(1)}, bf16[2,1,32,1,16,1,32]{6,3,2,5,4,1,0:T(2,128)(2,1)S(1)}, bf16[2,1,32,1,16,1,32]{6,3,2,5,4,...) fusion(bf16[3,2,33,2,17,2,32]{6,3,2,5,4,1,0:T(2,128)(2,1)} %res, ...), kind=kLoop, calls=%fused_computation.67 | loop fusion | bytes 2490368 | tf_op jit(solution)/shard_map/slice | solution.py:32
  65.6 5.1 %fusion.10 = (bf16[2,1,32,1,16,1,32]{6,3,2,5,4,1,0:T(2,128)(2,1)S(1)}, bf16[2,1,32,1,16,1,32]{6,3,2,5,4,1,0:T(2,128)(2,1)S(1)}, bf16[2,1,32,1,16,1,32]{6,3,2,5,4...) fusion(bf16[3,2,33,2,17,2,32]{6,3,2,5,4,1,0:T(2,128)(2,1)S(1)} , ...), kind=kLoop, calls=%fused_computation.68 | loop fusion | bytes 1048576 | tf_op jit(solution)/shard_map/slice | solution.py:32
  72.7 1.0 copy.161
  73.7 1.0 copy.162
  74.7 1.0 copy.163
  75.7 1.0 copy.164
  76.7 1.0 copy.165
  77.7 1.0 copy.166
  78.8 1.0 copy.167
  79.8 1.0 copy.168
  80.8 1.0 copy.169
  81.8 1.0 copy.170
  82.8 1.0 copy.171
  83.9 1.0 copy.172
  84.9 1.0 copy.173
  85.9 1.0 copy.154
  87.0 1.0 copy.147
  88.0 1.0 copy.148
  89.0 1.0 copy.149
  90.0 1.0 copy.150
  91.0 1.0 copy.151
  92.1 1.0 copy.152
  93.1 1.0 copy.153
  94.1 7.9 %concatenate.153 = bf16[1024,864]{1,0:T(8,128)(2,1)} concatenate(bf16[1024,32]{1,0:T(8,128)(2,1)} %bitcast.208, bf16[1024,32]{1,0:T(8,128)(2,1)} %bitcast.209, bf16[1024,32]{1,0:T(8,128)(2,1)} %bitcast.210, bf16[1024,32]{1,0:T(8,128)(2,1)} %bitcast.211, bf16[1024,32]{1,0:T(8,128)(2,1)} %bitcast.212, bf16[1024,32]{1,0:T(8,128)(2,1)} %bitcast.213, bf16[1024,32]{1,0:T(8,128)(2,1)} %bitcast.214, ...), dimensions={1} | concatenate | bytes 3538944 | tf_op jit(solution)/shard_map/concatenate | solution.py:34
  102.1 1.9 slice_add_fusion
  103.9 1.4 pad_maximum_fusion.4
  105.4 0.8 fusion.7
  106.4 4.8 %collective-permute-start.1 = (bf16[1,32,16,128]{3,0,2,1:T(2,128)(2,1)S(1)}, bf16[1,32,16,128]{3,0,2,1:T(2,128)(2,1)S(1)}, u32[]{:S(2)}, u32[]{:S(2)}) collective-permute-start(bf16[1,32,16,128]{3,0,2,1:T(2,128)(2,1)S(1)} %copy.174), channel_id=1, source_target_pairs={{0,1},{1,2},{2,3},{3,4},{4,5},{5,6},{6,7},{8,9},{9,10},{10,11},{11... | collective-permute-start | bytes 393224 | tf_op jit(solution)/shard_map/ppermute | solution.py:10
  111.5 3.3 %collective-permute-done.1 = bf16[1,32,16,128]{3,0,2,1:T(2,128)(2,1)S(1)} collective-permute-done((bf16[1,32,16,128]{3,0,2,1:T(2,128)(2,1)S(1)}, bf16[1,32,16,128]{3,0,2,1:T(2,128)(2,1)S(1)}, u32[]{:S(2)}, u32[]{:S(2)}) %collective-permute-start.1) | collective-permute-done | bytes 131104 | tf_op jit(solution)/shard_map/ppermute | solution.py:10
  114.9 0.6 fusion.5
  116.0 0.9 fusion.12
  117.5 2.5 convolution_bitcast_fusion
  119.9 5.2 %copy.190 = f32[256,3456]{1,0:T(8,128)} copy(f32[256,3456]{0,1:T(8,128)} %convolution_bitcast_fusion) | data formatting | bytes 7077888
  125.2 2.7 fusion.14
  128.0 78.8 %reduce-scatter.7.cloned.1.call-done = f32[32,3456]{1,0:T(8,128)} async-done(((f32[256,3456]{1,0:T(8,128)}), f32[32,3456]{1,0:T(8,128)}) %reduce-scatter.7.cloned.1.call-update) | async-done | bytes 442384
  206.8 2.8 copy.191
  210.1 0.5 broadcast.39
  210.6 0.7 reduce
  211.4 11.2 %all_to_all.33 = bf16[8,2,2048]{2,1,0:T(2,128)(2,1)S(1)} all-to-all(bf16[8,2,2048]{2,1,0:T(2,128)(2,1)S(1)} %reshape.227), channel_id=1, replica_groups=mesh['dp'=4,'space'=8] {'space'}, dimensions={0} | all-to-all | bytes 131072 | tf_op jit(solution)/shard_map/all_to_all | solution.py:96
  222.7 0.7 copy.187
  223.4 48.2 %reduce-scatter.5.cloned.1.call-done = f32[16,864]{1,0:T(8,128)} async-done(((f32[128,864]{1,0:T(8,128)}), f32[16,864]{1,0:T(8,128)}) %reduce-scatter.5.cloned.1.call-update) | async-done | bytes 55312 | tf_op jit(solution)/shard_map/reduce_scatter | solution.py:117
  271.6 12.4 %psum.16 = f32[16,864]{1,0:T(8,128)} all-reduce(f32[16,864]{1,0:T(8,128)} %reduce-scatter.5.cloned.1.call-done), channel_id=1, replica_groups=mesh['dp'=4,'space'=8] {'dp'}, use_global_device_ids=true, to_apply=%region_0.1 | all-reduce | flops 13824 | bytes 110592 | tf_op jit(solution)/shard_map/psum | solution.py:115
  284.0 35.4 %all-reduce.15.cloned.1.call-done = f32[32,3456]{0,1:T(8,128)} async-done(((f32[32,3456]{0,1:T(8,128)}), f32[32,3456]{0,1:T(8,128)}) %all-reduce.15.cloned.1.call-update) | async-done | bytes 442384 | tf_op jit(solution)/shard_map/psum | solution.py:115
  319.4 2.7 copy.188
  (70 shorter events, 5.3 us)
Async XLA Ops:
  7.2 15.9 %copy-start = (bf16[3456,256]{1,0:T(8,128)(2,1)S(1)}, bf16[3456,256]{1,0:T(8,128)(2,1)}, u32[]{:S(2)}) copy-start(bf16[3456,256]{1,0:T(8,128)(2,1)} %param.6) | copy-start | bytes 5308420
  8.8 14.2 %all-to-all-start.1 = ((bf16[32,8,128]{2,0,1:T(8,128)(2,1)}), bf16[32,8,128]{2,0,1:T(8,128)(2,1)S(1)}, u32[]{:S(2)}, u32[]{:S(2)}) async-start(bf16[32,8,128]{2,0,1:T(8,128)(2,1)} %bitcast.179), calls=%async_computation.1 | async-start | bytes 131072 | tf_op jit(solution)/shard_map/all_to_all | solution.py:97
  16.0 190.8 %reduce-scatter.7.cloned.1.call-start = ((), (), s32[]{:S(2)}) async-start(), calls=%async_computation.6 | async-start | bytes 3981312
  18.3 14.0 %collective-permute-start = (bf16[1,64,1024]{1,2,0:T(8,128)(2,1)}, bf16[1,64,1024]{1,2,0:T(8,128)(2,1)S(1)}, u32[]{:S(2)}, u32[]{:S(2)}) collective-permute-start(bf16[1,64,1024]{1,2,0:T(8,128)(2,1)} %slice_bitcast_fusion.9), channel_id=1, source_target_pairs={{0,1},{1,2},{2,3},{3,4},{4,5},{5,6},{6,7},{8,9},{9,10},{10,11},{11... | collective-permute-start | bytes 393224 | tf_op jit(solution)/shard_map/ppermute | solution.py:10
  28.6 1.0 copy-start.3
  30.8 71.2 %collective-permute-start.2 = (f32[1,32,16,128]{3,0,2,1:T(1,128)}, f32[1,32,16,128]{3,0,2,1:T(1,128)}, u32[]{:S(2)}, u32[]{:S(2)}) collective-permute-start(f32[1,32,16,128]{3,0,2,1:T(1,128)} %get-tuple-element.52), channel_id=1, source_target_pairs={{1,0},{2,1},{3,2},{4,3},{5,4},{6,5},{7,6},{9,8},{10,9},{11,10},{12... | collective-permute-start | bytes 786440 | tf_op jit(solution)/shard_map/ppermute | solution.py:10
  50.6 15.0 %copy-start.1 = (bf16[3,2,33,2,17,2,32]{6,3,2,5,4,1,0:T(2,128)(2,1)S(1)}, bf16[3,2,33,2,17,2,32]{6,3,2,5,4,1,0:T(2,128)(2,1)}, u32[]{:S(2)}) copy-start(bf16[3,2,33,2,17,2,32]{6,3,2,5,4,1,0:T(2,128)(2,1)} %reshape.213) | copy-start | bytes 2585092
  102.0 3.4 %copy-start.2 = (bf16[1024,864]{1,0:T(8,128)(2,1)S(1)}, bf16[1024,864]{1,0:T(8,128)(2,1)}, u32[]{:S(2)}) copy-start(bf16[1024,864]{1,0:T(8,128)(2,1)} %concatenate.153) | copy-start | bytes 5308420
  102.0 3.4 %copy-start.4 = (bf16[864,128]{1,0:T(8,128)(2,1)S(1)}, bf16[864,128]{1,0:T(8,128)(2,1)}, u32[]{:S(2)}) copy-start(bf16[864,128]{1,0:T(8,128)(2,1)} %param.5) | copy-start | bytes 663556
  106.4 8.4 %collective-permute-start.1 = (bf16[1,32,16,128]{3,0,2,1:T(2,128)(2,1)S(1)}, bf16[1,32,16,128]{3,0,2,1:T(2,128)(2,1)S(1)}, u32[]{:S(2)}, u32[]{:S(2)}) collective-permute-start(bf16[1,32,16,128]{3,0,2,1:T(2,128)(2,1)S(1)} %copy.174), channel_id=1, source_target_pairs={{0,1},{1,2},{2,3},{3,4},{4,5},{5,6},{6,7},{8,9},{9,10},{10,11},{11... | collective-permute-start | bytes 393224 | tf_op jit(solution)/shard_map/ppermute | solution.py:10
  125.1 146.5 %reduce-scatter.5.cloned.1.call-start = ((), (), s32[]{:S(2)}) async-start(), calls=%async_computation.4 | async-start | bytes 516096 | tf_op jit(solution)/shard_map/reduce_scatter | solution.py:117
  127.9 191.4 %all-reduce.15.cloned.1.call-start = ((), (), s32[]{:S(2)}) async-start(), calls=%async_computation.5 | async-start | bytes 3538944 | tf_op jit(solution)/shard_map/psum | solution.py:115
Sparse Core Ops, SparseCore 0:
  125.2 81.5 reduce-scatter.6
  210.1 61.4 reduce-scatter.4
  274.1 45.1 all-reduce.14
where the time goes:
time: 330 us; the launch traced here: 329 us
  waiting for transfers between devices  167 us (51%)
  local copies, waits for them, and re-layouts  92.2 us (28%)
  blocking collectives  23.6 us (7%)
  starting transfers between devices  17.5 us (5%)
  between operations  14.3 us (4%)
  other arithmetic  7.38 us (2%)
  matrix products  7.11 us (2%)
    unnamed x4, waiting for transfers between devices  78.9 us
    reduce_scatter x1, waiting for transfers between devices, on_device(): lax.psum_scatter(summed[0], 'space', scatter_dimension=0, tiled=True)  48.2 us
    slice x31, local copies, waits for them, and re-layouts, patches(): lax.slice(phased, start, limit).reshape(out_x, out_y, out_z, channels)  44.7 us
    psum x1, waiting for transfers between devices, on_device(): summed = lax.psum((term_one, term_two), 'dp')  35.4 us
    unnamed x47, local copies, waits for them, and re-layouts  20.1 us
    psum x1, blocking collectives, on_device(): summed = lax.psum((term_one, term_two), 'dp')  12.4 us
    all_to_all x1, blocking collectives, on_device(): lax.all_to_all(latent_slab, 'space', split_axis=0, concat_axis=1, tiled=T...  11.2 us
    ppermute x3, starting transfers between devices, from_behind(): return lax.ppermute(block, axis, route)  10.2 us
  transfers between devices with their start and end apart: 7, of which 5 were waited for; matrix products, arithmetic and copies ran while one was open for 26% of the time, Pallas kernels for 0%

commit v1 on v0

--- a/solution.py
+++ b/solution.py
@@ -94,7 +94,18 @@
     )
     latent_slab = latent_rows.reshape(quarter_x, -1, out_width).transpose(2, 0, 1)
     latent = lax.all_to_all(latent_slab, "space", split_axis=0, concat_axis=1, tiled=True)[None]
-    upstream = lax.all_to_all(cotangent[0], "space", split_axis=1, concat_axis=0, tiled=True)
+    ways, here = (lax.axis_size("space"), lax.axis_index("space"))
+    width = cotangent[0].shape[1] // ways
+    dims = list(cotangent[0].shape)
+    dims[1] = width
+    height = dims[0]
+    dims[0] = height * ways
+    upstream = jnp.zeros(dims, cotangent[0].dtype)
+    for mask in range(ways):
+        part = lax.dynamic_slice_in_dim(cotangent[0], (here ^ mask) * width, width, axis=1)
+        if mask:
+            part = lax.ppermute(part, "space", [(d, d ^ mask) for d in range(ways)])
+        upstream = lax.dynamic_update_slice_in_dim(upstream, part, (here ^ mask) * height, axis=0)
     grad_grid = upstream.transpose(1, 2, 0)
     grad_rows = grad_grid.reshape(-1, out_width)
     term_two = lax.dot_general(

time: 330 us -> 319 us (0.967)
  waiting for transfers between devices: 167 us -> 156 us
  local copies, waits for them, and re-layouts: 92.2 us -> 86.2 us
  starting transfers between devices: 17.5 us -> 22.5 us
    reduce_scatter x0 -> x1, waiting for transfers between devices: none -> 79.5 us  [on_device(): lax.psum_scatter(summed[1], 'space', scatter_dimension=0, tiled=True)]
    unnamed x4 -> x3, waiting for transfers between devices: 78.9 us -> 0.05 us
    psum x1, waiting for transfers between devices: 35.4 us -> 21.9 us  [on_device(): summed = lax.psum((term_one, term_two), 'dp')]
    ppermute x0 -> x7, starting transfers between devices: none -> 12.6 us  [on_device(): part = lax.ppermute(part, 'space', [(d, d ^ mask) for d in range(ways)])]
    unnamed x47 -> x52, local copies, waits for them, and re-layouts: 20.1 us -> 9.6 us
    all_to_all x1 -> x0, starting transfers between devices: 7.25 us -> none  [on_device(): lax.all_to_all(cotangent[0], 'space', split_axis=1, concat_axis=0, tiled=...]
  transfers between devices with their start and end apart: 7 -> 13, of which waited for: 5 -> 4; matrix products, arithmetic and copies ran while one was open for 26% -> 27% of each run, Pallas kernels for 0% -> 0%
where the time goes in v1:
time: 319 us; the launch traced here: 317 us
  waiting for transfers between devices  156 us (49%)
  local copies, waits for them, and re-layouts  86.2 us (27%)
  blocking collectives  23.3 us (7%)
  starting transfers between devices  22.5 us (7%)
  between operations  14.6 us (5%)
  other arithmetic  7.37 us (2%)
  matrix products  7.08 us (2%)
    reduce_scatter x1, waiting for transfers between devices, on_device(): lax.psum_scatter(summed[1], 'space', scatter_dimension=0, tiled=True)  79.5 us
    reduce_scatter x1, waiting for transfers between devices, on_device(): lax.psum_scatter(summed[0], 'space', scatter_dimension=0, tiled=True)  51.2 us
    slice x31, local copies, waits for them, and re-layouts, patches(): lax.slice(phased, start, limit).reshape(out_x, out_y, out_z, channels)  44.6 us
    psum x1, waiting for transfers between devices, on_device(): summed = lax.psum((term_one, term_two), 'dp')  21.9 us
    ppermute x7, starting transfers between devices, on_device(): part = lax.ppermute(part, 'space', [(d, d ^ mask) for d in range(ways)])  12.6 us
    psum x1, blocking collectives, on_device(): summed = lax.psum((term_one, term_two), 'dp')  12.4 us
    all_to_all x1, blocking collectives, on_device(): lax.all_to_all(latent_slab, 'space', split_axis=0, concat_axis=1, tiled=T...  11 us
    ppermute x3, starting transfers between devices, from_behind(): return lax.ppermute(block, axis, route)  9.83 us
  transfers between devices with their start and end apart: 13, of which 4 were waited for; matrix products, arithmetic and copies ran while one was open for 27% of the time, Pallas kernels for 0%

profile of v1, /device:TPU:0, one launch (start us, length us, event | category | flops | bytes accessed | tf_op | source)
XLA Modules:
  0.0 317.1 jit_solution(17448295521997678428)
XLA Ops:
  7.3 1.4 constant_dynamic-slice_fusion
  8.7 3.0 collective-permute-start.2
  11.7 1.6 collective-permute-start.3
  13.3 3.0 collective-permute-start.5
  16.3 1.3 collective-permute-start.6
  17.6 1.5 copy.185
  19.1 3.7 %collective-permute-start.7 = (bf16[32,1,128]{2,0,1:T(8,128)(2,1)S(1)}, bf16[32,1,128]{2,0,1:T(8,128)(2,1)S(1)}, u32[]{:S(2)}, u32[]{:S(2)}) collective-permute-start(bf16[32,1,128]{2,0,1:T(8,128)(2,1)S(1)} %bitcast.236), channel_id=1, source_target_pairs={{0,6},{1,7},{2,4},{3,5},{4,2},{5,3},{6,0},{7,1},{8,14},{9,15},{10,... | collective-permute-start | bytes 24584 | tf_op jit(solution)/shard_map/ppermute | solution.py:107
  23.5 0.4 dynamic_update_slice.25
  24.5 3.5 %collective-permute-start = (bf16[1,64,1024]{1,2,0:T(8,128)(2,1)S(1)}, bf16[1,64,1024]{1,2,0:T(8,128)(2,1)S(1)}, u32[]{:S(2)}, u32[]{:S(2)}) collective-permute-start(bf16[1,64,1024]{1,2,0:T(8,128)(2,1)S(1)} %slice_bitcast_fusion.9), channel_id=1, source_target_pairs={{0,1},{1,2},{2,3},{3,4},{4,5},{5,6},{6,7},{8,9},{9,10},{10,11},{11... | collective-permute-start | bytes 393224 | tf_op jit(solution)/shard_map/ppermute | solution.py:10
  30.5 0.7 convolution_bitcast_fusion
  32.5 1.0 copy.239
  33.5 0.6 slice_bitcast_fusion.8
  34.4 0.5 add_bitcast_fusion.2
  34.9 0.5 pad_maximum_fusion.3
  35.4 0.6 copy.240
  36.1 1.1 copy-done.3
  37.1 1.2 fusion.13
  38.3 1.5 collective-permute-start.9
  39.8 1.3 pad_maximum_fusion.2
  41.1 3.9 %copy.286 = bf16[5,64,32,32]{3,1,2,0:T(8,128)(2,1)} copy(bf16[5,64,32,32]{1,3,2,0:T(8,128)(2,1)} %pad_maximum_fusion.2) | data formatting | bytes 1310720
  45.0 4.9 %pad.74 = bf16[6,66,34,32]{3,1,2,0:T(8,128)(2,1)} pad(bf16[5,64,32,32]{3,1,2,0:T(8,128)(2,1)} %copy.286, bf16[]{:T(256)} %constant.15.clone.1), padding=0_1x1_1x1_1x0_0 | pad | bytes 1517058 | tf_op jit(solution)/shard_map/jit(_pad)/pad | solution.py:15
  50.0 8.2 %reshape.221 = bf16[3,2,33,2,17,2,32]{6,3,2,5,4,1,0:T(2,128)(2,1)} reshape(bf16[6,66,34,32]{3,1,2,0:T(8,128)(2,1)} %pad.74) | data formatting | bytes 1723392 | tf_op jit(solution)/shard_map/reshape | solution.py:16
  58.2 15.0 %fusion.11 = (bf16[2,1,32,1,16,1,32]{6,3,2,5,4,1,0:T(2,128)(2,1)S(1)}, bf16[2,1,32,1,16,1,32]{6,3,2,5,4,1,0:T(2,128)(2,1)S(1)}, bf16[2,1,32,1,16,1,32]{6,3,2,5,4...) fusion(bf16[3,2,33,2,17,2,32]{6,3,2,5,4,1,0:T(2,128)(2,1)} %res, ...), kind=kLoop, calls=%fused_computation.83 | loop fusion | bytes 2490368 | tf_op jit(solution)/shard_map/slice | solution.py:32
  73.3 5.1 %fusion.12 = (bf16[2,1,32,1,16,1,32]{6,3,2,5,4,1,0:T(2,128)(2,1)S(1)}, bf16[2,1,32,1,16,1,32]{6,3,2,5,4,1,0:T(2,128)(2,1)S(1)}, bf16[2,1,32,1,16,1,32]{6,3,2,5,4...) fusion(bf16[3,2,33,2,17,2,32]{6,3,2,5,4,1,0:T(2,128)(2,1)S(1)} , ...), kind=kLoop, calls=%fused_computation.84 | loop fusion | bytes 1048576 | tf_op jit(solution)/shard_map/slice | solution.py:32
  80.3 1.0 copy.202
  81.3 1.0 copy.203
  82.3 1.0 copy.204
  83.3 1.0 copy.205
  84.4 1.0 copy.206
  85.4 1.0 copy.207
  86.4 1.0 copy.208
  87.4 1.0 copy.209
  88.4 1.0 copy.210
  89.4 1.0 copy.211
  90.5 1.0 copy.212
  91.5 1.0 copy.213
  92.5 1.0 copy.214
  93.5 1.0 copy.195
  94.6 1.0 copy.188
  95.6 1.0 copy.189
  96.6 1.0 copy.190
  97.6 1.0 copy.191
  98.6 1.0 copy.192
  99.6 1.0 copy.193
  100.6 1.0 copy.194
  101.7 7.9 %concatenate.153 = bf16[1024,864]{1,0:T(8,128)(2,1)} concatenate(bf16[1024,32]{1,0:T(8,128)(2,1)} %bitcast.223, bf16[1024,32]{1,0:T(8,128)(2,1)} %bitcast.224, bf16[1024,32]{1,0:T(8,128)(2,1)} %bitcast.225, bf16[1024,32]{1,0:T(8,128)(2,1)} %bitcast.226, bf16[1024,32]{1,0:T(8,128)(2,1)} %bitcast.227, bf16[1024,32]{1,0:T(8,128)(2,1)} %bitcast.228, bf16[1024,32]{1,0:T(8,128)(2,1)} %bitcast.229, ...), dimensions={1} | concatenate | bytes 3538944 | tf_op jit(solution)/shard_map/concatenate | solution.py:34
  109.6 1.9 slice_add_fusion
  111.5 1.4 pad_maximum_fusion.4
  113.0 0.8 fusion.7
  114.0 4.8 %collective-permute-start.1 = (bf16[1,32,16,128]{3,0,2,1:T(2,128)(2,1)S(1)}, bf16[1,32,16,128]{3,0,2,1:T(2,128)(2,1)S(1)}, u32[]{:S(2)}, u32[]{:S(2)}) collective-permute-start(bf16[1,32,16,128]{3,0,2,1:T(2,128)(2,1)S(1)} %copy.215), channel_id=1, source_target_pairs={{0,1},{1,2},{2,3},{3,4},{4,5},{5,6},{6,7},{8,9},{9,10},{10,11},{11... | collective-permute-start | bytes 393224 | tf_op jit(solution)/shard_map/ppermute | solution.py:10
  119.1 3.3 %collective-permute-done.1 = bf16[1,32,16,128]{3,0,2,1:T(2,128)(2,1)S(1)} collective-permute-done((bf16[1,32,16,128]{3,0,2,1:T(2,128)(2,1)S(1)}, bf16[1,32,16,128]{3,0,2,1:T(2,128)(2,1)S(1)}, u32[]{:S(2)}, u32[]{:S(2)}) %collective-permute-start.1) | collective-permute-done | bytes 131104 | tf_op jit(solution)/shard_map/ppermute | solution.py:10
  122.4 0.6 fusion.5
  123.5 0.9 fusion.14
  125.0 2.4 fusion.8
  127.5 2.7 fusion.16
  130.4 79.5 %reduce-scatter.5.cloned.1.call-done = f32[32,3456]{1,0:T(8,128)} async-done(((f32[256,3456]{1,0:T(8,128)}), f32[32,3456]{1,0:T(8,128)}) %reduce-scatter.5.cloned.1.call-update) | async-done | bytes 442384 | tf_op jit(solution)/shard_map/reduce_scatter | solution.py:129
  210.3 0.5 broadcast.39
  210.8 0.7 reduce
  211.6 11.0 %all_to_all.15 = bf16[8,2,2048]{2,1,0:T(2,128)(2,1)S(1)} all-to-all(bf16[8,2,2048]{2,1,0:T(2,128)(2,1)S(1)} %reshape.233), channel_id=1, replica_groups=mesh['dp'=4,'space'=8] {'space'}, dimensions={0} | all-to-all | bytes 131072 | tf_op jit(solution)/shard_map/all_to_all | solution.py:96
  222.7 0.7 copy.243
  223.3 51.2 %reduce-scatter.3.cloned.1.call-done = f32[16,864]{1,0:T(8,128)} async-done(((f32[128,864]{1,0:T(8,128)}), f32[16,864]{1,0:T(8,128)}) %reduce-scatter.3.cloned.1.call-update) | async-done | bytes 55312 | tf_op jit(solution)/shard_map/reduce_scatter | solution.py:128
  274.6 12.4 %psum.16 = f32[16,864]{1,0:T(8,128)} all-reduce(f32[16,864]{1,0:T(8,128)} %reduce-scatter.3.cloned.1.call-done), channel_id=1, replica_groups=mesh['dp'=4,'space'=8] {'dp'}, use_global_device_ids=true, to_apply=%region_0.1 | all-reduce | flops 13824 | bytes 110592 | tf_op jit(solution)/shard_map/psum | solution.py:126
  286.9 21.9 %all-reduce.15.cloned.1.call-done = f32[32,3456]{1,0:T(8,128)} async-done(((f32[32,3456]{1,0:T(8,128)}), f32[32,3456]{1,0:T(8,128)}) %all-reduce.15.cloned.1.call-update) | async-done | bytes 442384 | tf_op jit(solution)/shard_map/psum | solution.py:126
  308.8 1.8 copy.366
  (104 shorter events, 9.2 us)
Async XLA Ops:
  7.2 23.4 %copy-start = (bf16[3456,256]{1,0:T(8,128)(2,1)S(1)}, bf16[3456,256]{1,0:T(8,128)(2,1)}, u32[]{:S(2)}) copy-start(bf16[3456,256]{1,0:T(8,128)(2,1)} %param.6) | copy-start | bytes 5308420
  7.2 202.7 %reduce-scatter.5.cloned.1.call-start = ((), (), s32[]{:S(2)}) async-start(), calls=%async_computation.4 | async-start | bytes 3981312 | tf_op jit(solution)/shard_map/reduce_scatter | solution.py:129
  8.7 10.4 %collective-permute-start.2 = (bf16[32,1,128]{2,0,1:T(8,128)(2,1)S(1)}, bf16[32,1,128]{2,0,1:T(8,128)(2,1)S(1)}, u32[]{:S(2)}, u32[]{:S(2)}) collective-permute-start(bf16[32,1,128]{2,0,1:T(8,128)(2,1)S(1)} %bitcast.241), channel_id=1, source_target_pairs={{0,1},{1,0},{2,3},{3,2},{4,5},{5,4},{6,7},{7,6},{8,9},{9,8},{10,11... | collective-permute-start | bytes 24584 | tf_op jit(solution)/shard_map/ppermute | solution.py:107
  11.7 11.1 %collective-permute-start.3 = (bf16[32,1,128]{2,0,1:T(8,128)(2,1)S(1)}, bf16[32,1,128]{2,0,1:T(8,128)(2,1)S(1)}, u32[]{:S(2)}, u32[]{:S(2)}) collective-permute-start(bf16[32,1,128]{2,0,1:T(8,128)(2,1)S(1)} %bitcast.240), channel_id=1, source_target_pairs={{0,2},{1,3},{2,0},{3,1},{4,6},{5,7},{6,4},{7,5},{8,10},{9,11},{10,... | collective-permute-start | bytes 24584 | tf_op jit(solution)/shard_map/ppermute | solution.py:107
  13.3 11.2 %collective-permute-start.4 = (bf16[32,1,128]{2,0,1:T(8,128)(2,1)S(1)}, bf16[32,1,128]{2,0,1:T(8,128)(2,1)S(1)}, u32[]{:S(2)}, u32[]{:S(2)}) collective-permute-start(bf16[32,1,128]{2,0,1:T(8,128)(2,1)S(1)} %bitcast.239), channel_id=1, source_target_pairs={{0,3},{1,2},{2,1},{3,0},{4,7},{5,6},{6,5},{7,4},{8,11},{9,10},{10,... | collective-permute-start | bytes 24584 | tf_op jit(solution)/shard_map/ppermute | solution.py:107
  13.3 15.3 %collective-permute-start.5 = (bf16[32,1,128]{2,0,1:T(8,128)(2,1)S(1)}, bf16[32,1,128]{2,0,1:T(8,128)(2,1)S(1)}, u32[]{:S(2)}, u32[]{:S(2)}) collective-permute-start(bf16[32,1,128]{2,0,1:T(8,128)(2,1)S(1)} %bitcast.238), channel_id=1, source_target_pairs={{0,4},{1,5},{2,6},{3,7},{4,0},{5,1},{6,2},{7,3},{8,12},{9,13},{10,... | collective-permute-start | bytes 24584 | tf_op jit(solution)/shard_map/ppermute | solution.py:107
  16.3 12.6 %collective-permute-start.6 = (bf16[32,1,128]{2,0,1:T(8,128)(2,1)S(1)}, bf16[32,1,128]{2,0,1:T(8,128)(2,1)S(1)}, u32[]{:S(2)}, u32[]{:S(2)}) collective-permute-start(bf16[32,1,128]{2,0,1:T(8,128)(2,1)S(1)} %bitcast.237), channel_id=1, source_target_pairs={{0,5},{1,4},{2,7},{3,6},{4,1},{5,0},{6,3},{7,2},{8,13},{9,12},{10,... | collective-permute-start | bytes 24584 | tf_op jit(solution)/shard_map/ppermute | solution.py:107
  19.1 10.3 %collective-permute-start.7 = (bf16[32,1,128]{2,0,1:T(8,128)(2,1)S(1)}, bf16[32,1,128]{2,0,1:T(8,128)(2,1)S(1)}, u32[]{:S(2)}, u32[]{:S(2)}) collective-permute-start(bf16[32,1,128]{2,0,1:T(8,128)(2,1)S(1)} %bitcast.236), channel_id=1, source_target_pairs={{0,6},{1,7},{2,4},{3,5},{4,2},{5,3},{6,0},{7,1},{8,14},{9,15},{10,... | collective-permute-start | bytes 24584 | tf_op jit(solution)/shard_map/ppermute | solution.py:107
  22.8 7.2 %collective-permute-start.8 = (bf16[32,1,128]{2,0,1:T(8,128)(2,1)S(1)}, bf16[32,1,128]{2,0,1:T(8,128)(2,1)S(1)}, u32[]{:S(2)}, u32[]{:S(2)}) collective-permute-start(bf16[32,1,128]{2,0,1:T(8,128)(2,1)S(1)} %bitcast.235), channel_id=1, source_target_pairs={{0,7},{1,6},{2,5},{3,4},{4,3},{5,2},{6,1},{7,0},{8,15},{9,14},{10,... | collective-permute-start | bytes 24584 | tf_op jit(solution)/shard_map/ppermute | solution.py:107
  24.5 15.3 %collective-permute-start = (bf16[1,64,1024]{1,2,0:T(8,128)(2,1)S(1)}, bf16[1,64,1024]{1,2,0:T(8,128)(2,1)S(1)}, u32[]{:S(2)}, u32[]{:S(2)}) collective-permute-start(bf16[1,64,1024]{1,2,0:T(8,128)(2,1)S(1)} %slice_bitcast_fusion.9), channel_id=1, source_target_pairs={{0,1},{1,2},{2,3},{3,4},{4,5},{5,6},{6,7},{8,9},{9,10},{10,11},{11... | collective-permute-start | bytes 393224 | tf_op jit(solution)/shard_map/ppermute | solution.py:10
  36.1 1.1 copy-start.3
  38.3 71.3 %collective-permute-start.9 = (f32[1,32,16,128]{3,0,2,1:T(1,128)}, f32[1,32,16,128]{3,0,2,1:T(1,128)}, u32[]{:S(2)}, u32[]{:S(2)}) collective-permute-start(f32[1,32,16,128]{3,0,2,1:T(1,128)} %get-tuple-element.49), channel_id=1, source_target_pairs={{1,0},{2,1},{3,2},{4,3},{5,4},{6,5},{7,6},{9,8},{10,9},{11,10},{12... | collective-permute-start | bytes 786440 | tf_op jit(solution)/shard_map/ppermute | solution.py:10
  58.2 15.0 %copy-start.1 = (bf16[3,2,33,2,17,2,32]{6,3,2,5,4,1,0:T(2,128)(2,1)S(1)}, bf16[3,2,33,2,17,2,32]{6,3,2,5,4,1,0:T(2,128)(2,1)}, u32[]{:S(2)}) copy-start(bf16[3,2,33,2,17,2,32]{6,3,2,5,4,1,0:T(2,128)(2,1)} %reshape.221) | copy-start | bytes 2585092
  109.6 3.4 %copy-start.2 = (bf16[1024,864]{1,0:T(8,128)(2,1)S(1)}, bf16[1024,864]{1,0:T(8,128)(2,1)}, u32[]{:S(2)}) copy-start(bf16[1024,864]{1,0:T(8,128)(2,1)} %concatenate.153) | copy-start | bytes 5308420
  109.6 3.4 %copy-start.4 = (bf16[864,128]{1,0:T(8,128)(2,1)S(1)}, bf16[864,128]{1,0:T(8,128)(2,1)}, u32[]{:S(2)}) copy-start(bf16[864,128]{1,0:T(8,128)(2,1)} %param.5) | copy-start | bytes 663556
  114.0 8.4 %collective-permute-start.1 = (bf16[1,32,16,128]{3,0,2,1:T(2,128)(2,1)S(1)}, bf16[1,32,16,128]{3,0,2,1:T(2,128)(2,1)S(1)}, u32[]{:S(2)}, u32[]{:S(2)}) collective-permute-start(bf16[1,32,16,128]{3,0,2,1:T(2,128)(2,1)S(1)} %copy.215), channel_id=1, source_target_pairs={{0,1},{1,2},{2,3},{3,4},{4,5},{5,6},{6,7},{8,9},{9,10},{10,11},{11... | collective-permute-start | bytes 393224 | tf_op jit(solution)/shard_map/ppermute | solution.py:10
  127.5 147.1 %reduce-scatter.3.cloned.1.call-start = ((), (), s32[]{:S(2)}) async-start(), calls=%async_computation.3 | async-start | bytes 516096 | tf_op jit(solution)/shard_map/reduce_scatter | solution.py:128
  130.3 178.5 %all-reduce.15.cloned.1.call-start = ((), (), s32[]{:S(2)}) async-start(), calls=%async_computation.5 | async-start | bytes 884736 | tf_op jit(solution)/shard_map/psum | solution.py:126
Sparse Core Ops, SparseCore 0:
  127.6 82.2 reduce-scatter.4
  213.1 61.3 reduce-scatter.2
  277.1 31.6 all-reduce.14
